TPU v7x, 128 devices: a whole 4x4x4 slice. The times are simulated.
128 devices in a mesh: tm: 4 (over x), mesh: 32 (over y, z, core).
Axes of the slice: x: 4, y: 4, z: 4, core: 2. Of those that a mesh axis runs over, the one named last changes fastest.
Arguments:
- right_sides: bfloat16 [8, 4096, 512], P('tm', 'mesh'), may hold values from -6 to 6
- diag_inverse: bfloat16 [8, 4096, 4096], P('tm', 'mesh'), may hold values from -0.09375 to 0.09375
- coupling: bfloat16 [8, 4096, 4096], P('tm', 'mesh'), may hold values from -0.0625 to 0.0625
- carry_in: bfloat16 [4096, 512], P('mesh'), may hold values from -6 to 6
- arrow_blocks: bfloat16 [8, 64, 4096], P('tm', None, 'mesh'), may hold values from -0.03125 to 0.03125
- tip_right: float32 [64, 512], replicated, may hold values from -6 to 6
- tip_inverse: float32 [64, 64], replicated, may hold values from -0.75 to 0.75
Outputs:
- forward_state: bfloat16 [8, 4096, 512], P('tm', 'mesh')
- tip_solution: float32 [64, 512], replicated
All inputs are finite; a program needn't handle non-finite values.
Results may differ from a plain program's by a relative error of at most 0.011.
Values may be sent and summed in bfloat16 or wider, within the bound.
A program may use at most 64 MiB of HBM per device.

v0:
```python
import jax
import jax.numpy as jnp
from jax import lax
from jax.sharding import PartitionSpec as P


def from_behind(block, axis, distance):
    devices = range(lax.axis_size(axis))
    route = [(i - distance, i) for i in devices if i - distance in devices]
    return lax.ppermute(block, axis, route)


def advance(matrix, source, earlier):
    coupled = jnp.dot(
        matrix,
        lax.all_gather(earlier, "mesh", axis=0, tiled=True),
        preferred_element_type=jnp.float32,
    )
    return (source - coupled).astype(jnp.bfloat16)


def body(right_sides, diag_inverse, coupling, carry_in, arrow_blocks, tip_right, tip_inverse):
    position = lax.axis_index("tm")
    devices_tm = lax.axis_size("tm")
    blocks, own_rows, columns = right_sides.shape
    scaled = jnp.einsum(
        "tij,tjr->tir",
        diag_inverse,
        lax.all_gather(right_sides, "mesh", axis=1, tiled=True),
        preferred_element_type=jnp.float32,
    )
    incoming = carry_in
    outputs = []
    for wave_step in range(devices_tm):
        current = incoming
        outputs = []
        for block_no in range(blocks):
            current = advance(coupling[block_no], scaled[block_no], current)
            outputs.append(current)
        if wave_step + 1 < devices_tm:
            moved = from_behind(current, "tm", 1)
            incoming = jnp.where(position == 0, carry_in, moved)
    solved = jnp.stack(outputs, axis=0)
    arrow_terms = jnp.einsum(
        "tfr,trs->fs", arrow_blocks, solved, preferred_element_type=jnp.float32
    )
    arrow_sum = lax.psum(arrow_terms, ("tm", "mesh"))
    tip_solution = jnp.dot(
        tip_inverse,
        tip_right - arrow_sum,
        precision=lax.Precision.HIGHEST,
        preferred_element_type=jnp.float32,
    )
    return (solved, tip_solution)


def solution(mesh):
    placed = (
        P("tm", "mesh", None),
        P("tm", "mesh", None),
        P("tm", "mesh", None),
        P("mesh", None),
        P("tm", None, "mesh"),
        P(),
        P(),
    )
    return jax.shard_map(
        body, mesh=mesh, in_specs=placed, out_specs=(P("tm", "mesh", None), P()), check_vma=False
    )
```

profile of v0, /device:TPU:1, one launch (start us, length us, event | category | flops | bytes accessed | tf_op | source)
XLA Modules:
  0.0 639.1 jit_solution(520782583988940051)
XLA Ops:
  7.2 0.0 all-gather.10.cloned.1.call-start
  7.2 0.7 all-gather.10.cloned.1.call-update
  7.9 0.0 all-gather.12.cloned.1.call-start
  8.0 0.7 all-gather.12.cloned.1.call-update
  8.7 0.0 all-gather.14.cloned.1.call-start
  8.7 58.4 %all-gather.10.cloned.1.call-done = bf16[2,4096,512]{2,1,0:T(8,128)(2,1)} async-done(((bf16[2,128,512]{2,1,0:T(8,128)(2,1)}), bf16[2,4096,512]{2,1,0:T(8,128)(2,1)}) %all-gather.10.cloned.1.call-update) | async-done | bytes 8388624 | tf_op jit(solution)/shard_map/all_gather | solution.py:29
  67.1 4.6 fusion.33
  71.8 43.6 %all-gather.12.cloned.1.call-done = bf16[4096,512]{1,0:T(8,128)(2,1)} async-done(((bf16[128,512]{1,0:T(8,128)(2,1)}), bf16[4096,512]{1,0:T(8,128)(2,1)}) %all-gather.12.cloned.1.call-update) | async-done | bytes 4194320 | tf_op jit(solution)/shard_map/all_gather | solution.py:16
  115.3 3.9 fusion.7
  119.2 0.0 all-gather.14.cloned.1.call-update
  119.2 0.0 all-gather.16.cloned.1.call-start
  119.3 45.8 %all-gather.14.cloned.1.call-done = bf16[4096,512]{1,0:T(8,128)(2,1)} async-done(((bf16[128,512]{1,0:T(8,128)(2,1)}), bf16[4096,512]{1,0:T(8,128)(2,1)}) %all-gather.14.cloned.1.call-update) | async-done | bytes 4194320 | tf_op jit(solution)/shard_map/all_gather | solution.py:16
  165.1 3.2 fusion.14
  168.3 3.1 collective-permute-start
  171.4 2.6 collective-permute-done
  174.0 0.7 broadcast_select_fusion.2
  174.7 0.0 all-gather.16.cloned.1.call-update
  174.7 0.0 all-gather.18.cloned.1.call-start
  174.8 47.6 %all-gather.16.cloned.1.call-done = bf16[4096,512]{1,0:T(8,128)(2,1)} async-done(((bf16[128,512]{1,0:T(8,128)(2,1)}), bf16[4096,512]{1,0:T(8,128)(2,1)}) %all-gather.16.cloned.1.call-update) | async-done | bytes 4194320 | tf_op jit(solution)/shard_map/all_gather | solution.py:16
  222.4 3.9 fusion.13
  226.3 0.0 all-gather.18.cloned.1.call-update
  226.3 0.0 all-gather.20.cloned.1.call-start
  226.4 45.8 %all-gather.18.cloned.1.call-done = bf16[4096,512]{1,0:T(8,128)(2,1)} async-done(((bf16[128,512]{1,0:T(8,128)(2,1)}), bf16[4096,512]{1,0:T(8,128)(2,1)}) %all-gather.18.cloned.1.call-update) | async-done | bytes 4194320 | tf_op jit(solution)/shard_map/all_gather | solution.py:16
  272.2 3.2 fusion.12
  275.4 3.1 collective-permute-start.1
  278.5 2.6 collective-permute-done.1
  281.1 0.7 broadcast_select_fusion.1
  281.8 0.0 all-gather.20.cloned.1.call-update
  281.8 0.0 all-gather.22.cloned.1.call-start
  281.9 47.6 %all-gather.20.cloned.1.call-done = bf16[4096,512]{1,0:T(8,128)(2,1)} async-done(((bf16[128,512]{1,0:T(8,128)(2,1)}), bf16[4096,512]{1,0:T(8,128)(2,1)}) %all-gather.20.cloned.1.call-update) | async-done | bytes 4194320 | tf_op jit(solution)/shard_map/all_gather | solution.py:16
  329.5 3.9 fusion.11
  333.4 0.0 all-gather.22.cloned.1.call-update
  333.4 0.0 all-gather.24.cloned.1.call-start
  333.4 45.8 %all-gather.22.cloned.1.call-done = bf16[4096,512]{1,0:T(8,128)(2,1)} async-done(((bf16[128,512]{1,0:T(8,128)(2,1)}), bf16[4096,512]{1,0:T(8,128)(2,1)}) %all-gather.22.cloned.1.call-update) | async-done | bytes 4194320 | tf_op jit(solution)/shard_map/all_gather | solution.py:16
  379.2 3.2 fusion.10
  382.5 3.1 collective-permute-start.2
  385.6 2.6 collective-permute-done.2
  388.2 0.7 broadcast_select_fusion
  388.9 0.0 all-gather.26.cloned.1.call-start
  389.0 47.6 %all-gather.24.cloned.1.call-done = bf16[4096,512]{1,0:T(8,128)(2,1)} async-done(((bf16[128,512]{1,0:T(8,128)(2,1)}), bf16[4096,512]{1,0:T(8,128)(2,1)}) %all-gather.24.cloned.1.call-update) | async-done | bytes 4194320 | tf_op jit(solution)/shard_map/all_gather | solution.py:16
  436.6 3.9 fusion.9
  440.5 0.0 all-gather.26.cloned.1.call-update
  440.5 0.0 all-reduce.2.cloned.1.call-start
  440.6 45.8 %all-gather.26.cloned.1.call-done = bf16[4096,512]{1,0:T(8,128)(2,1)} async-done(((bf16[128,512]{1,0:T(8,128)(2,1)}), bf16[4096,512]{1,0:T(8,128)(2,1)}) %all-gather.26.cloned.1.call-update) | async-done | bytes 4194320 | tf_op jit(solution)/shard_map/all_gather | solution.py:16
  486.4 3.2 fusion.15
  489.7 0.8 convolution_bitcast_fusion.7
  490.5 139.9 %all-reduce.2.cloned.1.call-done = f32[64,512]{1,0:T(8,128)} async-done(((f32[64,512]{1,0:T(8,128)}), f32[64,512]{1,0:T(8,128)}) %all-reduce.2.cloned.1.call-update) | async-done | bytes 131088 | tf_op jit(solution)/shard_map/psum | solution.py:47
  630.4 1.8 convolution_bitcast_fusion.8
  (17 shorter events, 0.1 us)
Async XLA Ops:
  7.2 60.0 %copy-start = (bf16[2,128,4096]{2,1,0:T(8,128)(2,1)S(1)}, bf16[2,128,4096]{2,1,0:T(8,128)(2,1)}, u32[]{:S(2)}) copy-start(bf16[2,128,4096]{2,1,0:T(8,128)(2,1)} %param.8) | copy-start | bytes 6291460
  7.2 59.9 %all-gather.10.cloned.1.call-start = ((), (), s32[]{:S(2)}) async-start(), calls=%async_computation | async-start | bytes 8650752 | tf_op jit(solution)/shard_map/all_gather | solution.py:29
  7.9 107.4 %all-gather.12.cloned.1.call-start = ((), (), s32[]{:S(2)}) async-start(), calls=%async_computation.1 | async-start | bytes 4325376 | tf_op jit(solution)/shard_map/all_gather | solution.py:16
  8.7 156.4 %all-gather.14.cloned.1.call-start = ((), (), s32[]{:S(2)}) async-start(), calls=%async_computation.2 | async-start | bytes 4325376 | tf_op jit(solution)/shard_map/all_gather | solution.py:16
  119.2 54.8 %copy-start.1 = (bf16[128,512]{1,0:T(8,128)(2,1)S(1)}, bf16[128,512]{1,0:T(8,128)(2,1)}, u32[]{:S(2)}) copy-start(bf16[128,512]{1,0:T(8,128)(2,1)} %param.10) | copy-start | bytes 393220
  119.2 103.2 %all-gather.16.cloned.1.call-start = ((), (), s32[]{:S(2)}) async-start(), calls=%async_computation.3 | async-start | bytes 4325376 | tf_op jit(solution)/shard_map/all_gather | solution.py:16
  168.3 5.7 collective-permute-start
  174.7 97.4 %all-gather.18.cloned.1.call-start = ((), (), s32[]{:S(2)}) async-start(), calls=%async_computation.4 | async-start | bytes 4325376 | tf_op jit(solution)/shard_map/all_gather | solution.py:16
  226.3 103.2 %all-gather.20.cloned.1.call-start = ((), (), s32[]{:S(2)}) async-start(), calls=%async_computation.5 | async-start | bytes 4325376 | tf_op jit(solution)/shard_map/all_gather | solution.py:16
  275.4 5.7 collective-permute-start.1
  281.8 97.4 %all-gather.22.cloned.1.call-start = ((), (), s32[]{:S(2)}) async-start(), calls=%async_computation.6 | async-start | bytes 4325376 | tf_op jit(solution)/shard_map/all_gather | solution.py:16
  333.4 103.2 %all-gather.24.cloned.1.call-start = ((), (), s32[]{:S(2)}) async-start(), calls=%async_computation.7 | async-start | bytes 4325376 | tf_op jit(solution)/shard_map/all_gather | solution.py:16
  382.5 5.7 collective-permute-start.2
  388.9 97.4 %all-gather.26.cloned.1.call-start = ((), (), s32[]{:S(2)}) async-start(), calls=%async_computation.8 | async-start | bytes 4325376 | tf_op jit(solution)/shard_map/all_gather | solution.py:16
  440.5 49.1 %copy-start.2 = (bf16[128,512]{1,0:T(8,128)(2,1)S(1)}, bf16[128,512]{1,0:T(8,128)(2,1)}, u32[]{:S(2)}) copy-start(bf16[128,512]{1,0:T(8,128)(2,1)} %fusion.9) | copy-start | bytes 393220
  440.5 49.2 %copy-start.5 = (bf16[2,64,128]{2,1,0:T(8,128)(2,1)S(1)}, bf16[2,64,128]{2,1,0:T(8,128)(2,1)}, u32[]{:S(2)}) copy-start(bf16[2,64,128]{2,1,0:T(8,128)(2,1)} %param.11) | copy-start | bytes 98308
  440.5 189.9 %copy-start.4 = (f32[64,512]{1,0:T(8,128)S(1)}, f32[64,512]{1,0:T(8,128)}, u32[]{:S(2)}) copy-start(f32[64,512]{1,0:T(8,128)} %param.12) | copy-start | bytes 393220
  440.5 189.9 %copy-start.6 = (f32[64,64]{1,0:T(8,128)S(1)}, f32[64,64]{1,0:T(8,128)}, u32[]{:S(2)}) copy-start(f32[64,64]{1,0:T(8,128)} %param.13) | copy-start | bytes 49156
  440.5 189.9 %all-reduce.2.cloned.1.call-start = ((), (), s32[]{:S(2)}) async-start(), calls=%async_computation.9 | async-start | bytes 262144 | tf_op jit(solution)/shard_map/psum | solution.py:47
  489.6 142.6 %copy-start.3 = (bf16[2,128,512]{2,1,0:T(8,128)(2,1)}, bf16[2,128,512]{2,1,0:T(8,128)(2,1)S(1)}, u32[]{:S(2)}) copy-start(bf16[2,128,512]{2,1,0:T(8,128)(2,1)S(1)} %pad_maximum_fusion) | copy-start | bytes 786436
Sparse Core Ops, SparseCore 0:
  10.4 56.6 all-gather.9
  69.4 45.8 all-gather.11
  119.4 45.6 all-gather.13
  174.8 47.5 all-gather.15
  226.4 45.6 all-gather.17
  281.9 47.4 all-gather.19
  333.5 45.6 all-gather.21
  389.0 47.5 all-gather.23
  440.6 45.6 all-gather.25
  491.5 138.8 all-reduce.1
where the time goes:
time: 639 us
  waiting for transfers between devices  577 us (90%)
  matrix products  35.8 us (6%)
  between operations  14.3 us (2%)
  starting transfers between devices  9.72 us (2%)
    all_gather x8, waiting for transfers between devices, advance(): lax.all_gather(earlier, 'mesh', axis=0, tiled=True)  370 us
    psum x1, waiting for transfers between devices, body(): arrow_sum = lax.psum(arrow_terms, ('tm', 'mesh'))  140 us
    all_gather x1, waiting for transfers between devices, body(): lax.all_gather(right_sides, 'mesh', axis=1, tiled=True)  58.4 us
    dot_general x8, matrix products, advance(): jnp.dot(matrix, lax.all_gather(earlier, 'mesh', axis=0, tiled=True), pref...  28.5 us
  transfers between devices with their start and end apart: 13, of which 13 were waited for; matrix products, arithmetic and copies ran while one was open for 1% of the time, Pallas kernels for 0%

commit v1 on v0

v1 whole, which is shorter than its diff:
```python
import functools

import jax
import jax.numpy as jnp
from jax import lax
from jax.experimental import pallas as pl
from jax.experimental.pallas import tpu as pltpu
from jax.sharding import PartitionSpec as P

MESH = pl.DeviceIdType.MESH
SIDE = 4
CHUNK = 32
AHEAD = 2


def device(x, y, z, core):
    return (lax.rem(x, SIDE), (lax.rem(y, SIDE) * SIDE + lax.rem(z, SIDE)) * 2 + core)


def times_transposed(rows, matrix):
    return lax.dot_general(
        rows, matrix, (((1,), (1,)), ((), ())), preferred_element_type=jnp.float32
    )


def kernel(
    rhs_ref, diag_ref, coup_ref, carry_ref, arrow_ref, tip_right_ref, tip_inverse_ref,
    out_ref, tip_ref,
    mats, own, gathered, arriving, part_a, part_b, send_a, send_b, recv_a, recv_b,
    state_a, state_b, arrow_own, turned, leaving, total, heard,
    mat_send, mat_recv, mat_local, sib_send, sib_recv,
    own_send, own_recv, vec_send, vec_recv, vec_local,
    a_send, a_recv, b_send, b_recv, next_send, next_recv,
    arrow_send, arrow_recv, out_send, out_recv, sum_send, sum_recv, tip_send, tip_recv,
):
    x = lax.axis_index("tm")
    place = lax.axis_index("mesh")
    y, z, core = place // (2 * SIDE), lax.rem(place // 2, SIDE), lax.rem(place, 2)
    other = 1 - core
    shard = rhs_ref.shape[1]
    chip = 2 * shard
    span = SIDE * chip
    lane = rhs_ref.shape[2] // 2
    chunks = lane // CHUNK
    sibling = device(x, y, z, other)
    along_z = lambda r: device(x, y, z + r, core)
    along_y = lambda r: device(x, y + r, z, core)
    along_x = lambda r: device(x + r, y, z, core)
    steps = range(1, SIDE)

    def aligned(value, unit):
        return pl.multiple_of(value, unit)

    def remote(src, dst, send, recv, target):
        return pltpu.make_async_remote_copy(
            src_ref=src, dst_ref=dst, send_sem=send, recv_sem=recv,
            device_id=target, device_id_type=MESH,
        )

    barrier = pltpu.get_barrier_semaphore()
    neighbours = [f(r) for f in (along_z, along_y, along_x) for r in steps] + [sibling]
    for target in neighbours:
        pl.semaphore_signal(barrier, inc=1, device_id=target, device_id_type=MESH)
    pl.semaphore_wait(barrier, len(neighbours))

    sources = (diag_ref.at[0], coup_ref.at[0], diag_ref.at[1], coup_ref.at[1])
    lines = (along_z, along_z, along_y, along_y)
    mine = (z, z, y, y)

    def block_of(m, at, half):
        return mats.at[m, pl.ds(aligned(at * chip + half * shard, shard), shard), :]

    def pieces(m, r):
        target_at = lax.rem(mine[m] + r, SIDE)
        rows = pl.ds(aligned(mine[m] * chip + core * shard, shard), shard)
        if m < 2:
            return [
                (
                    sources[m].at[:, pl.ds(aligned(a * span + target_at * chip, chip), chip)],
                    mats.at[m, rows, pl.ds(a * chip, chip)],
                )
                for a in range(SIDE)
            ]
        return [
            (
                sources[m].at[:, pl.ds(aligned(target_at * span, span), span)],
                mats.at[m, rows, :],
            )
        ]

    def send_matrix(m):
        for r in steps:
            for src, dst in pieces(m, r):
                remote(src, dst, mat_send.at[m, r], mat_recv.at[m, r], lines[m](r)).start()
        for src, dst in pieces(m, 0):
            remote(src, dst, sib_send.at[m, 0], sib_recv.at[m, 0], sibling).start()
            pltpu.make_async_copy(src, dst, mat_local.at[m]).start()

    def forward_copy(m, r):
        block = block_of(m, lax.rem(mine[m] - r + SIDE, SIDE), core)
        return remote(block, block, sib_send.at[m, r], sib_recv.at[m, r], sibling)

    def whole(m, r, half):
        return block_of(m, lax.rem(mine[m] - r + SIDE, SIDE), half)

    def arrive(*which):
        for r in (1, 3, 2):
            for m in which:
                remote(
                    whole(m, r, core), whole(m, r, core), mat_send.at[m, r], mat_recv.at[m, r], lines[m](r)
                ).wait_recv()
                forward_copy(m, r).start()
        for m in which:
            pltpu.make_async_copy(whole(m, 0, core), whole(m, 0, core), mat_local.at[m]).wait()
            for r in range(SIDE):
                remote(
                    whole(m, r, other), whole(m, r, other), sib_send.at[m, r], sib_recv.at[m, r], sibling
                ).wait_recv()

    send_matrix(0)
    send_matrix(1)

    vectors = (rhs_ref.at[0], carry_ref, rhs_ref.at[1])
    targets = (gathered.at[0], arriving, gathered.at[1])
    vec_lines = (along_y, along_y, along_z)
    vec_mine = (y, y, z)
    own_half = pl.ds(aligned(core * shard, shard), shard)

    def own_copy(v):
        return remote(
            turned.at[v], own.at[v, :, own_half], own_send.at[v], own_recv.at[v], sibling
        )

    def other_copy(v):
        half = own.at[v, :, pl.ds(aligned(other * shard, shard), shard)]
        return remote(half, half, own_send.at[v], own_recv.at[v], sibling)

    def turn(v):
        value = vectors[v][:, pl.ds(aligned(core * lane, lane), lane)]
        own[v, :, own_half] = value.T
        value = vectors[v][:, pl.ds(aligned(other * lane, lane), lane)]
        turned[v] = value.T
        own_copy(v).start()

    arrow_half = arrow_own.at[:, :, own_half]
    arrow_other = arrow_own.at[:, :, pl.ds(aligned(other * shard, shard), shard)]

    def vec_copy(v, r):
        slot = targets[v].at[:, pl.ds(aligned(vec_mine[v] * chip, chip), chip)]
        return remote(own.at[v], slot, vec_send.at[v, r], vec_recv.at[v, r], vec_lines[v](r))

    def vec_own(v):
        slot = targets[v].at[:, pl.ds(aligned(vec_mine[v] * chip, chip), chip)]
        return pltpu.make_async_copy(own.at[v], slot, vec_local.at[v])

    def vec_wait(v):
        for r in steps:
            at = lax.rem(vec_mine[v] - r + SIDE, SIDE)
            slot = targets[v].at[:, pl.ds(aligned(at * chip, chip), chip)]
            remote(slot, slot, vec_send.at[v, r], vec_recv.at[v, r], vec_lines[v](r)).wait_recv()
        vec_own(v).wait()

    def vec_start(v):
        other_copy(v).wait_recv()
        for r in steps:
            vec_copy(v, r).start()
        vec_own(v).start()

    turn(0)

    @pl.when(x == 0)
    def _():
        turn(1)

    turn(2)
    arrow_own[:, :, own_half] = arrow_ref[...]
    remote(arrow_ref, arrow_half, arrow_send, arrow_recv, sibling).start()
    vec_start(0)

    @pl.when(x == 0)
    def _():
        vec_start(1)

    vec_start(2)
    send_matrix(2)
    send_matrix(3)

    arrive(0, 1)
    vec_wait(0)
    part_a[...] = times_transposed(gathered[0], mats[0])

    @pl.when(x == 0)
    def _():
        vec_wait(1)

    def rows_of(k):
        return pl.ds(aligned(k * CHUNK, CHUNK), CHUNK)

    def chunk_copy(src, dst, send, recv, line, k, r):
        return remote(
            src.at[rows_of(k)], dst.at[r - 1, rows_of(k)], send.at[k, r], recv.at[k, r], line(r)
        )

    copy_a = functools.partial(chunk_copy, send_a, recv_a, a_send, a_recv, along_z)
    copy_b = functools.partial(chunk_copy, send_b, recv_b, b_send, b_recv, along_y)

    def copy_next(k):
        return remote(
            state_b.at[rows_of(k)], arriving.at[rows_of(k)], next_send.at[k], next_recv.at[k], along_x(1)
        )

    def spread(part, sent, matrix, source, copy, k):
        rows = rows_of(k)
        value = part[rows, :] - times_transposed(source[rows, :], matrix[...])
        part[rows, :] = value
        sent[rows, :] = value.astype(jnp.bfloat16)
        for r in (2, 1, 3):
            copy(k, r).start()

    def settle(part, received, state, copy, k):
        rows = rows_of(k)
        for r in (1, 3, 2):
            copy(k, r).wait_recv()
        value = part[rows, :]
        for r in steps:
            value = value + received[r - 1, rows, :].astype(jnp.float32)
        state[rows, :] = value.astype(jnp.bfloat16)

    def first(k):
        @pl.when(x > 0)
        def _():
            copy_next(k).wait_recv()

        spread(part_a, send_a, mats.at[1], arriving, copy_a, k)

    def second(k):
        settle(part_a, recv_a, state_a, copy_a, k)
        spread(part_b, send_b, mats.at[3], state_a, copy_b, k)

    def third(k):
        settle(part_b, recv_b, state_b, copy_b, k)

        @pl.when(x < SIDE - 1)
        def _():
            copy_next(k).start()

    def lead(k, carry):
        first(k)
        return carry

    lax.fori_loop(0, AHEAD, lead, 0)
    arrive(2, 3)
    vec_wait(2)
    part_b[...] = times_transposed(gathered[1], mats[2])

    def step(n, carry):
        @pl.when(n >= 2 * AHEAD)
        def _():
            third(n - 2 * AHEAD)

        @pl.when(n < chunks + AHEAD)
        def _():
            second(n - AHEAD)

        @pl.when(n < chunks)
        def _():
            first(n)

        return carry

    lax.fori_loop(AHEAD, chunks + 2 * AHEAD, step, 0)

    remote(arrow_other, arrow_other, arrow_send, arrow_recv, sibling).wait_recv()
    rows_a = pl.ds(aligned(z * chip, chip), chip)
    rows_b = pl.ds(aligned(y * chip, chip), chip)
    total[0] = times_transposed(arrow_own[0], state_a[:, rows_a]) + times_transposed(
        arrow_own[1], state_b[:, rows_b]
    )

    def sum_copy(phase, r):
        line = (along_z, along_y, along_x)[phase]
        return remote(
            total.at[phase], heard.at[phase, r - 1], sum_send.at[phase, r], sum_recv.at[phase, r], line(r)
        )

    def sum_wait(phase):
        for r in steps:
            sum_copy(phase, r).wait_recv()
        value = total[phase]
        for r in steps:
            value = value + heard[phase, r - 1]
        return value

    for r in steps:
        sum_copy(0, r).start()

    own_columns = pl.ds(aligned(core * lane, lane), lane)

    back = [(state_a, z), (state_b, y)]

    def out_copy(b, columns):
        return remote(
            leaving.at[b], out_ref.at[b, :, columns], out_send.at[b], out_recv.at[b], sibling
        )

    total[1] = sum_wait(0)
    for r in steps:
        sum_copy(1, r).start()

    for b, (state, at) in enumerate(back):
        start = at * chip
        leaving[b] = state[:, pl.ds(aligned(start + other * shard, shard), shard)].T
        out_copy(b, own_columns).start()
        out_ref[b, :, own_columns] = state[:, pl.ds(aligned(start + core * shard, shard), shard)].T

    total[2] = sum_wait(1)
    for r in steps:
        sum_copy(2, r).start()
    full = sum_wait(2)
    tip = jnp.dot(
        tip_inverse_ref[...],
        tip_right_ref[:, own_columns] - full,
        precision=lax.Precision.HIGHEST,
        preferred_element_type=jnp.float32,
    )
    total[3] = tip
    tip_copy = remote(total.at[3], tip_ref.at[:, own_columns], tip_send, tip_recv, sibling)
    tip_copy.start()
    tip_ref[:, own_columns] = tip

    for m in range(4):
        for r in steps:
            remote(whole(m, r, core), whole(m, r, core), mat_send.at[m, r], mat_recv.at[m, r], lines[m](r)).wait_send()
        for r in range(SIDE):
            forward_copy(m, r).wait_send()
    def vec_drain(v):
        own_copy(v).wait_send()
        for r in steps:
            vec_copy(v, r).wait_send()

    vec_drain(0)
    pl.when(x == 0)(lambda: vec_drain(1))
    vec_drain(2)

    remote(arrow_ref, arrow_half, arrow_send, arrow_recv, sibling).wait_send()

    def drain(k, carry):
        for r in steps:
            copy_a(k, r).wait_send()
            copy_b(k, r).wait_send()

        @pl.when(x < SIDE - 1)
        def _():
            copy_next(k).wait_send()

        return carry

    lax.fori_loop(0, chunks, drain, 0)
    for phase in range(3):
        for r in steps:
            sum_copy(phase, r).wait_send()
    other_columns = pl.ds(aligned(other * lane, lane), lane)
    for b in range(2):
        out_copy(b, own_columns).wait_send()
        out_copy(b, other_columns).wait_recv()
    tip_copy.wait_send()
    remote(total.at[3], tip_ref.at[:, other_columns], tip_send, tip_recv, sibling).wait_recv()


def body(right_sides, diag_inverse, coupling, carry_in, arrow_blocks, tip_right, tip_inverse):
    blocks, shard, columns = right_sides.shape
    effects = tip_right.shape[0]
    chip, span, lane = 2 * shard, 2 * shard * SIDE, columns // 2
    chunks = lane // CHUNK
    vmem = pl.BlockSpec(memory_space=pltpu.VMEM)
    hbm = pl.BlockSpec(memory_space=pl.ANY)
    half, full = jnp.bfloat16, jnp.float32
    dma = pltpu.SemaphoreType.DMA
    return pl.pallas_call(
        kernel,
        out_shape=(
            jax.ShapeDtypeStruct(right_sides.shape, half),
            jax.ShapeDtypeStruct(tip_right.shape, full),
        ),
        in_specs=[vmem, hbm, hbm, vmem, vmem, vmem, vmem],
        out_specs=(vmem, vmem),
        scratch_shapes=[
            pltpu.VMEM((4, span, span), half),
            pltpu.VMEM((3, lane, chip), half),
            pltpu.VMEM((2, lane, span), half),
            pltpu.VMEM((lane, span), half),
            pltpu.VMEM((lane, span), full),
            pltpu.VMEM((lane, span), full),
            pltpu.VMEM((lane, span), half),
            pltpu.VMEM((lane, span), half),
            pltpu.VMEM((SIDE - 1, lane, span), half),
            pltpu.VMEM((SIDE - 1, lane, span), half),
            pltpu.VMEM((lane, span), half),
            pltpu.VMEM((lane, span), half),
            pltpu.VMEM((blocks, effects, chip), half),
            pltpu.VMEM((3, lane, shard), half),
            pltpu.VMEM((blocks, shard, lane), half),
            pltpu.VMEM((4, effects, lane), full),
            pltpu.VMEM((3, SIDE - 1, effects, lane), full),
            dma((4, SIDE)), dma((4, SIDE)), dma((4,)), dma((4, SIDE)), dma((4, SIDE)),
            dma((3,)), dma((3,)), dma((3, SIDE)), dma((3, SIDE)), dma((3,)),
            dma((chunks, SIDE)), dma((chunks, SIDE)), dma((chunks, SIDE)), dma((chunks, SIDE)),
            dma((chunks,)), dma((chunks,)),
            dma, dma, dma((2,)), dma((2,)), dma((3, SIDE)), dma((3, SIDE)), dma, dma,
        ],
        compiler_params=pltpu.CompilerParams(
            collective_id=0, has_side_effects=True, vmem_limit_bytes=48 << 20
        ),
    )(right_sides, diag_inverse, coupling, carry_in, arrow_blocks, tip_right, tip_inverse)


def solution(mesh):
    placed = (
        P("tm", "mesh", None),
        P("tm", "mesh", None),
        P("tm", "mesh", None),
        P("mesh", None),
        P("tm", None, "mesh"),
        P(),
        P(),
    )
    return jax.shard_map(
        body, mesh=mesh, in_specs=placed, out_specs=(P("tm", "mesh", None), P()), check_vma=False
    )
```

time: 639 us -> 155 us (0.24)
  waiting for transfers between devices: 577 us -> 0 us
  Pallas kernels: 0 us -> 145 us
  matrix products: 35.8 us -> 0 us
  between operations: 14.3 us -> 0.66 us
  starting transfers between devices: 9.72 us -> 0 us
  local copies, waits for them, and re-layouts: 0.03 us -> 8.81 us
    all_gather x9 -> x0, waiting for transfers between devices: 428 us -> none  [the longest x8 370 us: advance(): lax.all_gather(earlier, 'mesh', axis=0, tiled=True)]
    pallas_call x0 -> x1, Pallas kernels: none -> 145 us  [body(): pl.pallas_call(kernel, out_shape=(jax.ShapeDtypeStruct(right_sides.shape,...]
    psum x1 -> x0, waiting for transfers between devices: 140 us -> none  [body(): arrow_sum = lax.psum(arrow_terms, ('tm', 'mesh'))]
    dot_general x11 -> x0, matrix products: 35.8 us -> none  [the longest x8 28.5 us: advance(): jnp.dot(matrix, lax.all_gather(earlier, 'mesh', axis=0, tiled=True), pref...]
    ppermute x3 -> x0, starting transfers between devices: 9.32 us -> none  [from_behind(): return lax.ppermute(block, axis, route)]
    unnamed x14 -> x16, local copies, waits for them, and re-layouts: 0.03 us -> 8.81 us
    ppermute x3 -> x0, waiting for transfers between devices: 7.83 us -> none  [from_behind(): return lax.ppermute(block, axis, route)]
  transfers between devices with their start and end apart: 13 -> 0, of which waited for: 13 -> 0; matrix products, arithmetic and copies ran while one was open for 1% -> 0% of each run, Pallas kernels for 0% -> 0%
where the time goes in v1:
time: 155 us
  Pallas kernels  145 us (94%)
  local copies, waits for them, and re-layouts  8.81 us (6%)
    pallas_call x1, Pallas kernels, body(): pl.pallas_call(kernel, out_shape=(jax.ShapeDtypeStruct(right_sides.shape,...  145 us
    unnamed x16, local copies, waits for them, and re-layouts  8.81 us

profile of v1, /device:TPU:1, one launch (start us, length us, event | category | flops | bytes accessed | tf_op | source)
XLA Modules:
  0.0 154.8 jit_solution(16437710645302582076)
XLA Ops:
  0.6 0.0 copy-start
  0.6 1.6 %copy-done = bf16[2,128,4096]{2,1,0:T(8,128)(2,1)S(1)} copy-done((bf16[2,128,4096]{2,1,0:T(8,128)(2,1)S(1)}, bf16[2,128,4096]{2,1,0:T(8,128)(2,1)}, u32[]{:S(2)}) %copy-start) | copy-done | bytes 2097176
  2.2 0.0 copy-start.1
  2.2 1.6 %copy-done.1 = bf16[2,128,4096]{2,1,0:T(8,128)(2,1)S(1)} copy-done((bf16[2,128,4096]{2,1,0:T(8,128)(2,1)S(1)}, bf16[2,128,4096]{2,1,0:T(8,128)(2,1)}, u32[]{:S(2)}) %copy-start.1) | copy-done | bytes 2097176
  3.8 0.0 copy-start.2
  3.8 0.9 copy-done.2
  4.8 0.0 copy-start.3
  4.8 0.9 copy-done.3
  5.7 0.0 copy-start.4
  5.7 0.9 copy-done.4
  6.6 0.0 copy-start.5
  6.6 0.8 copy-done.5
  7.3 0.0 copy-start.6
  7.3 0.8 copy-done.6
  8.1 145.4 %shard_map.86 = (bf16[2,128,512]{2,1,0:T(8,128)(2,1)S(1)}, f32[64,512]{1,0:T(8,128)S(1)}) custom-call(bf16[2,128,512]{2,1,0:T(8,128)(2,1)S(1)} %copy-done.2, bf16[2,128,4096]{2,1,0:T(8,128)(2,1)S(1)} %copy-done, bf16[2,128,4096]{2,1,0:T(8,128)(2,1)S(1)} %copy-done.1, bf16[128,512]{1,0:T(8,128)(2,1)S(1)} %copy-done.3, bf16[2,64,128]{2,1,0:T(8,128)(2,1)S(1)} %copy-done.5, ...), custom_call_target="tpu_custom_call" | custom-call | tf_op jit(solution)/shard_map/pallas_call | solution.py:379
  153.5 0.7 copy.11
  154.2 0.7 copy.12
Async XLA Ops:
  0.6 1.6 %copy-start = (bf16[2,128,4096]{2,1,0:T(8,128)(2,1)S(1)}, bf16[2,128,4096]{2,1,0:T(8,128)(2,1)}, u32[]{:S(2)}) copy-start(bf16[2,128,4096]{2,1,0:T(8,128)(2,1)} %diag_ref.1) | copy-start | bytes 6291460
  2.2 1.6 %copy-start.1 = (bf16[2,128,4096]{2,1,0:T(8,128)(2,1)S(1)}, bf16[2,128,4096]{2,1,0:T(8,128)(2,1)}, u32[]{:S(2)}) copy-start(bf16[2,128,4096]{2,1,0:T(8,128)(2,1)} %coup_ref.1) | copy-start | bytes 6291460
  3.8 0.9 copy-start.2
  4.8 0.9 copy-start.3
  5.7 0.9 copy-start.4
  6.6 0.8 copy-start.5
  7.3 0.8 copy-start.6

commit v2 on v1

v2 whole, which is shorter than its diff:
```python
import functools

import jax
import jax.numpy as jnp
from jax import lax
from jax.experimental import pallas as pl
from jax.experimental.pallas import tpu as pltpu
from jax.sharding import PartitionSpec as P

MESH = pl.DeviceIdType.MESH
SIDE = 4
CHUNK = 16
VMEM_LIMIT = 63 << 20
AHEAD = 3


def device(x, y, z, core):
    return (lax.rem(x, SIDE), (lax.rem(y, SIDE) * SIDE + lax.rem(z, SIDE)) * 2 + core)


def times_transposed(rows, matrix):
    return lax.dot_general(
        rows, matrix, (((1,), (1,)), ((), ())), preferred_element_type=jnp.float32
    )


def kernel(
    rhs_hbm, diag_ref, coup_ref, carry_hbm, arrow_hbm, tip_right_hbm, tip_inverse_hbm,
    out_ref, tip_ref,
    rhs_ref, carry_ref, arrow_ref, tip_right_ref, tip_inverse_ref,
    mats, gathered, arriving, part_a, part_b, send_a, send_b, recv_a, recv_b,
    state_a, state_b, arrow_line, turned, leaving, line_sum, line_heard, plane_sum, plane_heard,
    load_sem, mat_send, mat_recv, mat_local, sib_send, sib_recv,
    turn_send, turn_recv, vec_send, vec_recv,
    a_send, a_recv, b_send, b_recv, next_send, next_recv,
    arrow_sib_send, arrow_sib_recv, arrow_send, arrow_recv, arrow_local,
    out_send, out_recv, line_send, line_recv, plane_send, plane_recv,
):
    x = lax.axis_index("tm")
    place = lax.axis_index("mesh")
    y, z, core = place // (2 * SIDE), lax.rem(place // 2, SIDE), lax.rem(place, 2)
    other = 1 - core
    shard = rhs_ref.shape[1]
    chip = 2 * shard
    span = SIDE * chip
    lane = rhs_ref.shape[2] // 2
    chunks = lane // CHUNK
    effects = tip_ref.shape[0]
    sibling = device(x, y, z, other)
    along_z = lambda r: device(x, y, z + r, core)
    along_y = lambda r: device(x, y + r, z, core)
    along_x = lambda r: device(x + r, y, z, core)
    across_x = lambda r: device(x + r, y, z, other)
    steps = range(1, SIDE)

    loads = [
        pltpu.make_async_copy(src, dst, load_sem.at[i])
        for i, (src, dst) in enumerate((
            (rhs_hbm, rhs_ref), (carry_hbm, carry_ref), (arrow_hbm, arrow_ref),
            (tip_right_hbm, tip_right_ref), (tip_inverse_hbm, tip_inverse_ref),
        ))
    ]
    for load in loads:
        load.start()

    def aligned(value, unit):
        return pl.multiple_of(value, unit)

    def remote(src, dst, send, recv, target):
        return pltpu.make_async_remote_copy(
            src_ref=src, dst_ref=dst, send_sem=send, recv_sem=recv,
            device_id=target, device_id_type=MESH,
        )

    barrier = pltpu.get_barrier_semaphore()
    neighbours = [f(r) for f in (along_z, along_y, along_x, across_x) for r in steps]
    neighbours.append(sibling)
    for target in neighbours:
        pl.semaphore_signal(barrier, inc=1, device_id=target, device_id_type=MESH)

    vectors = (lambda: rhs_ref[0], lambda: carry_ref[...], lambda: rhs_ref[1])
    targets = (gathered.at[0], arriving, gathered.at[1])
    vec_lines = (along_y, along_y, along_z)
    vec_mine = (y, y, z)

    def slot(v, at, half):
        return targets[v].at[:, pl.ds(aligned(at * chip + half * shard, shard), shard)]

    def turn(v):
        value = vectors[v]().T
        mine = jnp.where(core == 0, value[:lane], value[lane:])
        slot(v, vec_mine[v], core)[...] = mine
        turned[v] = jnp.where(core == 0, value[lane:], value[:lane])

    loads[0].wait()
    loads[1].wait()
    turn(0)

    @pl.when(x == 0)
    def _():
        turn(1)

    turn(2)
    pl.semaphore_wait(barrier, len(neighbours))

    sources = (diag_ref.at[0], coup_ref.at[0], diag_ref.at[1], coup_ref.at[1])
    lines = (along_z, along_z, along_y, along_y)
    mine = (z, z, y, y)

    def pieces(m, r):
        target_at = lax.rem(mine[m] + r, SIDE)
        rows = pl.ds(aligned(mine[m] * chip + core * shard, shard), shard)
        if m < 2:
            return [
                (
                    sources[m].at[:, pl.ds(aligned(a * span + target_at * chip, chip), chip)],
                    mats.at[m, rows, pl.ds(a * chip, chip)],
                )
                for a in range(SIDE)
            ]
        return [
            (
                sources[m].at[:, pl.ds(aligned(target_at * span, span), span)],
                mats.at[m, rows, :],
            )
        ]

    def send_matrix(m):
        for r in (2, 1, 3):
            for src, dst in pieces(m, r):
                remote(src, dst, mat_send.at[m, r], mat_recv.at[m, r], lines[m](r)).start()

    def send_local(m):
        for src, dst in pieces(m, 0):
            remote(src, dst, sib_send.at[m, 0], sib_recv.at[m, 0], sibling).start()
            pltpu.make_async_copy(src, dst, mat_local.at[m]).start()

    def block(m, r, half):
        at = lax.rem(mine[m] - r + SIDE, SIDE)
        return mats.at[m, pl.ds(aligned(at * chip + half * shard, shard), shard), :]

    def line_copy(m, r):
        rows = block(m, r, core)
        return remote(rows, rows, mat_send.at[m, r], mat_recv.at[m, r], lines[m](r))

    def sibling_copy(m, r, half):
        rows = block(m, r, half)
        return remote(rows, rows, sib_send.at[m, r], sib_recv.at[m, r], sibling)

    def forward(m):
        for r in (1, 3, 2):
            line_copy(m, r).wait_recv()
            sibling_copy(m, r, core).start()

    def complete(m):
        rows = block(m, 0, core)
        pltpu.make_async_copy(rows, rows, mat_local.at[m]).wait()
        for r in range(SIDE):
            sibling_copy(m, r, other).wait_recv()

    def turn_copy(v):
        return remote(
            turned.at[v], slot(v, vec_mine[v], core), turn_send.at[v], turn_recv.at[v], sibling
        )

    def vec_copy(v, r, half):
        rows = slot(v, vec_mine[v], half)
        return remote(
            rows, rows, vec_send.at[v, r, half], vec_recv.at[v, r, half], vec_lines[v](r)
        )

    def vec_begin(v):
        turn_copy(v).start()
        for r in (2, 1, 3):
            vec_copy(v, r, core).start()

    def vec_rest(v):
        rows = slot(v, vec_mine[v], other)
        remote(rows, rows, turn_send.at[v], turn_recv.at[v], sibling).wait_recv()
        for r in (2, 1, 3):
            vec_copy(v, r, other).start()

    def vec_wait(v):
        for r in (1, 3, 2):
            for half in range(2):
                rows = slot(v, lax.rem(vec_mine[v] - r + SIDE, SIDE), half)
                remote(
                    rows, rows, vec_send.at[v, r, half], vec_recv.at[v, r, half], vec_lines[v](r)
                ).wait_recv()

    arrow_lines = (along_z, along_y)
    arrow_mine = (z, y)

    def arrow_slot(b, at, half):
        return arrow_line.at[b, :, pl.ds(aligned(at * chip + half * shard, shard), shard)]

    def arrow_local_copy(b):
        return pltpu.make_async_copy(
            arrow_ref.at[b], arrow_slot(b, arrow_mine[b], core), arrow_local.at[b]
        )

    def arrow_sibling_copy(b, half):
        return remote(
            arrow_ref.at[b], arrow_slot(b, arrow_mine[b], half),
            arrow_sib_send.at[b], arrow_sib_recv.at[b], sibling,
        )

    def arrow_copy(b, r, at):
        rows = arrow_line.at[b, :, pl.ds(aligned(at * chip, chip), chip)]
        return remote(rows, rows, arrow_send.at[b, r], arrow_recv.at[b, r], arrow_lines[b](r))

    vec_begin(0)

    @pl.when(x == 0)
    def _():
        vec_begin(1)

    send_matrix(0)
    send_matrix(1)
    turn_copy(2).start()
    send_local(0)
    send_local(1)
    vec_rest(0)

    @pl.when(x == 0)
    def _():
        vec_rest(1)

    send_matrix(2)
    send_matrix(3)
    send_local(2)
    send_local(3)
    loads[2].wait()
    for b in range(2):
        arrow_local_copy(b).start()
        arrow_sibling_copy(b, core).start()

    forward(0)
    vec_wait(0)
    complete(0)
    part_a[...] = times_transposed(gathered[0], mats[0])
    forward(1)
    for r in (2, 1, 3):
        vec_copy(2, r, core).start()
    vec_rest(2)
    complete(1)

    @pl.when(x == 0)
    def _():
        vec_wait(1)

    def rows_of(k):
        return pl.ds(aligned(k * CHUNK, CHUNK), CHUNK)

    def chunk_copy(src, dst, send, recv, line, k, r):
        return remote(
            src.at[rows_of(k)], dst.at[r - 1, rows_of(k)], send.at[k, r], recv.at[k, r], line(r)
        )

    copy_a = functools.partial(chunk_copy, send_a, recv_a, a_send, a_recv, along_z)
    copy_b = functools.partial(chunk_copy, send_b, recv_b, b_send, b_recv, along_y)

    def copy_next(k):
        return remote(
            state_b.at[rows_of(k)], arriving.at[rows_of(k)], next_send.at[k], next_recv.at[k], along_x(1)
        )

    def spread(part, sent, matrix, source, copy, k):
        rows = rows_of(k)
        value = part[rows, :] - times_transposed(source[rows, :], matrix[...])
        part[rows, :] = value
        sent[rows, :] = value.astype(jnp.bfloat16)
        for r in (2, 1, 3):
            copy(k, r).start()

    def settle(part, received, state, copy, k):
        rows = rows_of(k)
        for r in (1, 3, 2):
            copy(k, r).wait_recv()
        value = part[rows, :]
        for r in steps:
            value = value + received[r - 1, rows, :].astype(jnp.float32)
        state[rows, :] = value.astype(jnp.bfloat16)

    def first(k):
        @pl.when(x > 0)
        def _():
            copy_next(k).wait_recv()

        spread(part_a, send_a, mats.at[1], arriving, copy_a, k)

    def second(k):
        settle(part_a, recv_a, state_a, copy_a, k)
        spread(part_b, send_b, mats.at[3], state_a, copy_b, k)

    def third(k):
        settle(part_b, recv_b, state_b, copy_b, k)

        @pl.when(x < SIDE - 1)
        def _():
            copy_next(k).start()

    def second_block():
        forward(2)
        forward(3)
        vec_wait(2)
        complete(2)
        part_b[...] = times_transposed(gathered[1], mats[2])
        complete(3)
        for b in range(2):
            arrow_sibling_copy(b, other).wait_recv()
            arrow_local_copy(b).wait()
            for r in steps:
                arrow_copy(b, r, arrow_mine[b]).start()

    pl.when(x > 0)(second_block)

    def lead(k, carry):
        first(k)
        return carry

    lax.fori_loop(0, AHEAD, lead, 0)
    pl.when(x == 0)(second_block)

    def step(n, carry):
        @pl.when(n >= 2 * AHEAD)
        def _():
            third(n - 2 * AHEAD)

        @pl.when(jnp.logical_and(n >= AHEAD, n < chunks + AHEAD))
        def _():
            second(n - AHEAD)

        @pl.when(n < chunks)
        def _():
            first(n)

        return carry

    sum_lines = (along_y, along_z)
    half_lane = lane // 2

    def line_copy_of(b, h, r):
        return remote(
            line_sum.at[b, h], line_heard.at[b, h, r - 1],
            line_send.at[b, h, r], line_recv.at[b, h, r], sum_lines[b](r),
        )

    def line_begin(b, h):
        state = (state_a, state_b)[b]
        line_sum[b, h] = times_transposed(
            arrow_line[b], state[pl.ds(h * half_lane, half_lane), :]
        )
        for r in (2, 1, 3):
            line_copy_of(b, h, r).start()

    def plane_targets(h):
        found = []
        for r in range(SIDE):
            if r:
                found.append((0, r, along_x(r)))
            found.append((1, r, across_x(r) if r else sibling))
        return [
            remote(
                plane_sum.at[h], plane_heard.at[h, cross, r],
                plane_send.at[h, cross, r], plane_recv.at[h, cross, r], target,
            )
            for cross, r, target in found
        ]

    def plane_begin(h):
        value = jnp.zeros((effects, half_lane), jnp.float32)
        for b in range(2):
            value = value + line_sum[b, h]
            for r in steps:
                line_copy_of(b, h, r).wait_recv()
                value = value + line_heard[b, h, r - 1]
        plane_sum[h] = value
        for copy in plane_targets(h):
            copy.start()

    middle = chunks // 2 + 2 * AHEAD
    lax.fori_loop(AHEAD, middle, step, 0)
    for b in range(2):
        for r in steps:
            arrow_copy(b, r, lax.rem(arrow_mine[b] - r + SIDE, SIDE)).wait_recv()
    line_begin(0, 0)
    line_begin(1, 0)
    lax.fori_loop(middle, chunks + 2 * AHEAD, step, 0)
    line_begin(1, 1)
    line_begin(0, 1)
    plane_begin(0)

    def out_copy(b, columns):
        return remote(
            leaving.at[b], out_ref.at[b, :, columns], out_send.at[b], out_recv.at[b], sibling
        )

    own_columns = pl.ds(aligned(core * lane, lane), lane)
    other_columns = pl.ds(aligned(other * lane, lane), lane)
    for b, (state, at) in enumerate([(state_a, z), (state_b, y)]):
        start = at * chip
        leaving[b] = state[:, pl.ds(aligned(start + other * shard, shard), shard)].T
        out_copy(b, own_columns).start()
        out_ref[b, :, own_columns] = state[:, pl.ds(aligned(start + core * shard, shard), shard)].T

    plane_begin(1)

    for m in range(4):
        for r in steps:
            line_copy(m, r).wait_send()
        for r in range(SIDE):
            sibling_copy(m, r, core).wait_send()

    def vec_drain(v):
        turn_copy(v).wait_send()
        for r in steps:
            for half in range(2):
                vec_copy(v, r, half).wait_send()

    vec_drain(0)
    pl.when(x == 0)(lambda: vec_drain(1))
    vec_drain(2)
    for b in range(2):
        arrow_sibling_copy(b, core).wait_send()
        for r in steps:
            arrow_copy(b, r, arrow_mine[b]).wait_send()

    def drain(k, carry):
        for r in steps:
            copy_a(k, r).wait_send()
            copy_b(k, r).wait_send()

        @pl.when(x < SIDE - 1)
        def _():
            copy_next(k).wait_send()

        return carry

    lax.fori_loop(0, chunks, drain, 0)
    for b in range(2):
        out_copy(b, own_columns).wait_send()
        out_copy(b, other_columns).wait_recv()
        for h in range(2):
            for r in steps:
                line_copy_of(b, h, r).wait_send()
    loads[3].wait()
    loads[4].wait()

    for h in range(2):
        for copy in plane_targets(h):
            copy.wait_send()
            copy.wait_recv()
        for cross, owner in enumerate((core, other)):
            value = plane_heard[h, 1, 0] if cross else plane_sum[h]
            for r in steps:
                value = value + plane_heard[h, cross, r]
            columns = pl.ds(aligned(owner * lane + h * half_lane, half_lane), half_lane)
            tip_ref[:, columns] = jnp.dot(
                tip_inverse_ref[...],
                tip_right_ref[:, columns] - value,
                precision=lax.Precision.HIGHEST,
                preferred_element_type=jnp.float32,
            )


def body(right_sides, diag_inverse, coupling, carry_in, arrow_blocks, tip_right, tip_inverse):
    blocks, shard, columns = right_sides.shape
    effects = tip_right.shape[0]
    chip, span, lane = 2 * shard, 2 * shard * SIDE, columns // 2
    chunks = lane // CHUNK
    vmem = pl.BlockSpec(memory_space=pltpu.VMEM)
    hbm = pl.BlockSpec(memory_space=pl.ANY)
    half, full = jnp.bfloat16, jnp.float32
    dma = pltpu.SemaphoreType.DMA
    return pl.pallas_call(
        kernel,
        out_shape=(
            jax.ShapeDtypeStruct(right_sides.shape, half),
            jax.ShapeDtypeStruct(tip_right.shape, full),
        ),
        in_specs=[hbm] * 7,
        out_specs=(vmem, vmem),
        scratch_shapes=[
            pltpu.VMEM(right_sides.shape, half),
            pltpu.VMEM(carry_in.shape, half),
            pltpu.VMEM(arrow_blocks.shape, half),
            pltpu.VMEM(tip_right.shape, full),
            pltpu.VMEM(tip_inverse.shape, full),
            pltpu.VMEM((4, span, span), half),
            pltpu.VMEM((2, lane, span), half),
            pltpu.VMEM((lane, span), half),
            pltpu.VMEM((lane, span), full),
            pltpu.VMEM((lane, span), full),
            pltpu.VMEM((lane, span), half),
            pltpu.VMEM((lane, span), half),
            pltpu.VMEM((SIDE - 1, lane, span), half),
            pltpu.VMEM((SIDE - 1, lane, span), half),
            pltpu.VMEM((lane, span), half),
            pltpu.VMEM((lane, span), half),
            pltpu.VMEM((blocks, effects, span), half),
            pltpu.VMEM((3, lane, shard), half),
            pltpu.VMEM((blocks, shard, lane), half),
            pltpu.VMEM((2, 2, effects, lane // 2), full),
            pltpu.VMEM((2, 2, SIDE - 1, effects, lane // 2), full),
            pltpu.VMEM((2, effects, lane // 2), full),
            pltpu.VMEM((2, 2, SIDE, effects, lane // 2), full),
            dma((5,)), dma((4, SIDE)), dma((4, SIDE)), dma((4,)), dma((4, SIDE)), dma((4, SIDE)),
            dma((3,)), dma((3,)), dma((3, SIDE, 2)), dma((3, SIDE, 2)),
            dma((chunks, SIDE)), dma((chunks, SIDE)), dma((chunks, SIDE)), dma((chunks, SIDE)),
            dma((chunks,)), dma((chunks,)),
            dma((2,)), dma((2,)), dma((2, SIDE)), dma((2, SIDE)), dma((2,)),
            dma((2,)), dma((2,)), dma((2, 2, SIDE)), dma((2, 2, SIDE)), dma((2, 2, SIDE)), dma((2, 2, SIDE)),
        ],
        compiler_params=pltpu.CompilerParams(
            collective_id=0, has_side_effects=True, vmem_limit_bytes=VMEM_LIMIT
        ),
    )(right_sides, diag_inverse, coupling, carry_in, arrow_blocks, tip_right, tip_inverse)


def solution(mesh):
    placed = (
        P("tm", "mesh", None),
        P("tm", "mesh", None),
        P("tm", "mesh", None),
        P("mesh", None),
        P("tm", None, "mesh"),
        P(),
        P(),
    )
    return jax.shard_map(
        body, mesh=mesh, in_specs=placed, out_specs=(P("tm", "mesh", None), P()), check_vma=False
    )
```

time: 155 us -> 138 us (0.89)
  Pallas kernels: 145 us -> 133 us
  local copies, waits for them, and re-layouts: 8.81 us -> 3.24 us
    pallas_call x1, Pallas kernels: 145 us -> 133 us  [body(): pl.pallas_call(kernel, out_shape=(jax.ShapeDtypeStruct(right_sides.shape,...]
    unnamed x16 -> x2, local copies, waits for them, and re-layouts: 8.81 us -> 3.24 us
where the time goes in v2:
time: 138 us; the launch traced here: 137 us
  Pallas kernels  133 us (96%)
  local copies, waits for them, and re-layouts  3.24 us (2%)
    pallas_call x1, Pallas kernels, body(): pl.pallas_call(kernel, out_shape=(jax.ShapeDtypeStruct(right_sides.shape,...  133 us
    unnamed x2, local copies, waits for them, and re-layouts  3.24 us

profile of v2, /device:TPU:1, one launch (start us, length us, event | category | flops | bytes accessed | tf_op | source)
XLA Modules:
  0.0 137.4 jit_solution(10859592877465732229)
XLA Ops:
  0.6 133.5 %shard_map.86 = (bf16[2,128,512]{2,1,0:T(8,128)(2,1)}, f32[64,512]{1,0:T(8,128)}) custom-call(bf16[2,128,512]{2,1,0:T(8,128)(2,1)} %rhs_hbm.1, bf16[2,128,4096]{2,1,0:T(8,128)(2,1)} %diag_ref.1, bf16[2,128,4096]{2,1,0:T(8,128)(2,1)} %coup_ref.1, bf16[128,512]{1,0:T(8,128)(2,1)} %carry_hbm.1, bf16[2,64,128]{2,1,0:T(8,128)(2,1)} %arrow_hbm.1, ...), custom_call_target="tpu_custom_call" | custom-call | tf_op jit(solution)/shard_map/pallas_call | solution.py:476
  134.1 1.7 %copy.11 = bf16[2,128,512]{2,1,0:T(8,128)(2,1)} copy(bf16[2,128,512]{2,1,0:T(8,128)(2,1)} %get-tuple-element.4) | data formatting | bytes 524288
  135.8 1.6 %copy.12 = f32[64,512]{1,0:T(8,128)} copy(f32[64,512]{1,0:T(8,128)} %get-tuple-element.5) | data formatting | bytes 262144

commit v3 on v2

--- a/solution.py
+++ b/solution.py
@@ -11,7 +11,7 @@
 SIDE = 4
 CHUNK = 16
 VMEM_LIMIT = 63 << 20
-AHEAD = 3
+AHEAD = 4
 
 
 def device(x, y, z, core):
@@ -29,8 +29,9 @@
     out_ref, tip_ref,
     rhs_ref, carry_ref, arrow_ref, tip_right_ref, tip_inverse_ref,
     mats, gathered, arriving, part_a, part_b, send_a, send_b, recv_a, recv_b,
-    state_a, state_b, arrow_line, turned, leaving, line_sum, line_heard, plane_sum, plane_heard,
+    state_a, state_b, flipped, relay, relay_carry, arrow_line, turned, leaving, line_sum, line_heard, plane_sum, plane_heard,
     load_sem, mat_send, mat_recv, mat_local, sib_send, sib_recv,
+    relay_recv, relay_send, carry_recv, carry_send,
     turn_send, turn_recv, vec_send, vec_recv,
     a_send, a_recv, b_send, b_recv, next_send, next_recv,
     arrow_sib_send, arrow_sib_recv, arrow_send, arrow_recv, arrow_local,
@@ -63,6 +64,9 @@
     for load in loads:
         load.start()
 
+    helper = jnp.logical_or(x == 1, x == 3)
+    part = x // 2
+
     def aligned(value, unit):
         return pl.multiple_of(value, unit)
 
@@ -74,33 +78,37 @@
 
     barrier = pltpu.get_barrier_semaphore()
     neighbours = [f(r) for f in (along_z, along_y, along_x, across_x) for r in steps]
-    neighbours.append(sibling)
+    neighbours += [sibling]
+    neighbours += [device(x + d, y + a, z + b, core) for d in (1, 3) for a, b in ((0, 2), (2, 0))]
     for target in neighbours:
         pl.semaphore_signal(barrier, inc=1, device_id=target, device_id_type=MESH)
 
-    vectors = (lambda: rhs_ref[0], lambda: carry_ref[...], lambda: rhs_ref[1])
-    targets = (gathered.at[0], arriving, gathered.at[1])
+    half_lane = lane // 2
+    targets = (gathered.at[0], relay_carry, gathered.at[1])
     vec_lines = (along_y, along_y, along_z)
     vec_mine = (y, y, z)
 
     def slot(v, at, half):
         return targets[v].at[:, pl.ds(aligned(at * chip + half * shard, shard), shard)]
 
-    def turn(v):
-        value = vectors[v]().T
-        mine = jnp.where(core == 0, value[:lane], value[lane:])
+    def leaves(v):
+        return turned.at[v, pl.ds(0, half_lane)] if v == 1 else turned.at[v]
+
+    def turn(v, value):
+        value = value.T
+        mine, theirs = value[:lane], value[lane:]
+        if v == 1:
+            mine = jnp.where(part == 0, mine[:half_lane], mine[half_lane:])
+            theirs = jnp.where(part == 0, theirs[:half_lane], theirs[half_lane:])
+        mine, theirs = jnp.where(core == 0, mine, theirs), jnp.where(core == 0, theirs, mine)
         slot(v, vec_mine[v], core)[...] = mine
-        turned[v] = jnp.where(core == 0, value[lane:], value[:lane])
+        leaves(v)[...] = theirs
 
     loads[0].wait()
     loads[1].wait()
-    turn(0)
-
-    @pl.when(x == 0)
-    def _():
-        turn(1)
-
-    turn(2)
+    turn(0, rhs_ref[0])
+    pl.when(helper)(lambda: turn(1, carry_ref[...]))
+    turn(2, rhs_ref[1])
     pl.semaphore_wait(barrier, len(neighbours))
 
     sources = (diag_ref.at[0], coup_ref.at[0], diag_ref.at[1], coup_ref.at[1])
@@ -125,10 +133,36 @@
             )
         ]
 
-    def send_matrix(m):
-        for r in (2, 1, 3):
+    def send_near(m):
+        for r in (1, 3):
             for src, dst in pieces(m, r):
                 remote(src, dst, mat_send.at[m, r], mat_recv.at[m, r], lines[m](r)).start()
+
+    def send_far(m):
+        for src, dst in pieces(m, 2):
+            remote(src, dst, mat_send.at[m, 2], mat_recv.at[m, 2], lines[m](2)).start()
+
+    def send_round(m):
+        rows = shard // 2
+        found = pieces(m, 2)
+        width = span // len(found)
+        for n, (src, _) in enumerate(found):
+            columns = pl.ds(n * width, width)
+            for h, d in enumerate((1, 3)):
+                target = device(x + d, y, z + 2, core) if m < 2 else device(x + d, y + 2, z, core)
+                remote(
+                    src.at[pl.ds(h * rows, rows)], relay.at[m, :, columns],
+                    mat_send.at[m, 2], relay_recv.at[m], target,
+                ).start()
+
+    def pass_on(m):
+        rows = shard // 2
+        at = lax.rem(mine[m] + 2, SIDE)
+        dst = mats.at[m, pl.ds(aligned(at * chip + core * shard + part * rows, rows), rows), :]
+        return remote(relay.at[m], dst, relay_send.at[m], mat_recv.at[m, 2], device(0, y, z, core))
+
+    def relay_wait(m):
+        remote(relay.at[m], relay.at[m], relay_send.at[m], relay_recv.at[m], device(0, y, z, core)).wait_recv()
 
     def send_local(m):
         for src, dst in pieces(m, 0):
@@ -147,20 +181,29 @@
         rows = block(m, r, half)
         return remote(rows, rows, sib_send.at[m, r], sib_recv.at[m, r], sibling)
 
+    def flip(m, r, half):
+        if m % 2:
+            at = lax.rem(mine[m] - r + SIDE, SIDE)
+            columns = pl.ds(aligned(at * chip + half * shard, shard), shard)
+            flipped[m // 2, :, columns] = block(m, r, half)[...].T
+
     def forward(m):
         for r in (1, 3, 2):
             line_copy(m, r).wait_recv()
             sibling_copy(m, r, core).start()
+            flip(m, r, core)
 
     def complete(m):
         rows = block(m, 0, core)
         pltpu.make_async_copy(rows, rows, mat_local.at[m]).wait()
-        for r in range(SIDE):
+        flip(m, 0, core)
+        for r in (0, 1, 3, 2):
             sibling_copy(m, r, other).wait_recv()
+            flip(m, r, other)
 
     def turn_copy(v):
         return remote(
-            turned.at[v], slot(v, vec_mine[v], core), turn_send.at[v], turn_recv.at[v], sibling
+            leaves(v), slot(v, vec_mine[v], core), turn_send.at[v], turn_recv.at[v], sibling
         )
 
     def vec_copy(v, r, half):
@@ -210,26 +253,52 @@
         return remote(rows, rows, arrow_send.at[b, r], arrow_recv.at[b, r], arrow_lines[b](r))
 
     vec_begin(0)
+    pl.when(helper)(lambda: vec_begin(1))
+    for m in range(2):
+        send_near(m)
 
     @pl.when(x == 0)
     def _():
-        vec_begin(1)
-
-    send_matrix(0)
-    send_matrix(1)
+        for m in range(2):
+            send_round(m)
+
     turn_copy(2).start()
-    send_local(0)
-    send_local(1)
     vec_rest(0)
+    pl.when(helper)(lambda: vec_rest(1))
+    for m in range(2, 4):
+        send_near(m)
 
     @pl.when(x == 0)
     def _():
-        vec_rest(1)
-
-    send_matrix(2)
-    send_matrix(3)
-    send_local(2)
-    send_local(3)
+        for m in range(2, 4):
+            send_round(m)
+
+    for m in range(4):
+        send_local(m)
+
+    def carry_copy(p):
+        return remote(
+            relay_carry, arriving.at[pl.ds(p * half_lane, half_lane)],
+            carry_send, carry_recv.at[p], device(0, y, z, core),
+        )
+
+    @pl.when(helper)
+    def _():
+        for m in range(2):
+            relay_wait(m)
+            pass_on(m).start()
+        vec_wait(1)
+        for p in range(2):
+            pl.when(part == p)(carry_copy(p).start)
+        for m in range(2, 4):
+            relay_wait(m)
+            pass_on(m).start()
+
+    @pl.when(x > 0)
+    def _():
+        for m in range(4):
+            send_far(m)
+
     loads[2].wait()
     for b in range(2):
         arrow_local_copy(b).start()
@@ -247,7 +316,8 @@
 
     @pl.when(x == 0)
     def _():
-        vec_wait(1)
+        for p in range(2):
+            carry_copy(p).wait_recv()
 
     def rows_of(k):
         return pl.ds(aligned(k * CHUNK, CHUNK), CHUNK)
@@ -265,19 +335,21 @@
             state_b.at[rows_of(k)], arriving.at[rows_of(k)], next_send.at[k], next_recv.at[k], along_x(1)
         )
 
-    def spread(part, sent, matrix, source, copy, k):
+    def spread(terms, sent, matrix, source, copy, k):
         rows = rows_of(k)
-        value = part[rows, :] - times_transposed(source[rows, :], matrix[...])
-        part[rows, :] = value
+        value = terms[rows, :] - jnp.dot(
+            source[rows, :], matrix[...], preferred_element_type=jnp.float32
+        )
+        terms[rows, :] = value
         sent[rows, :] = value.astype(jnp.bfloat16)
         for r in (2, 1, 3):
             copy(k, r).start()
 
-    def settle(part, received, state, copy, k):
+    def settle(terms, received, state, copy, k):
         rows = rows_of(k)
         for r in (1, 3, 2):
             copy(k, r).wait_recv()
-        value = part[rows, :]
+        value = terms[rows, :]
         for r in steps:
             value = value + received[r - 1, rows, :].astype(jnp.float32)
         state[rows, :] = value.astype(jnp.bfloat16)
@@ -287,11 +359,11 @@
         def _():
             copy_next(k).wait_recv()
 
-        spread(part_a, send_a, mats.at[1], arriving, copy_a, k)
+        spread(part_a, send_a, flipped.at[0], arriving, copy_a, k)
 
     def second(k):
         settle(part_a, recv_a, state_a, copy_a, k)
-        spread(part_b, send_b, mats.at[3], state_a, copy_b, k)
+        spread(part_b, send_b, flipped.at[1], state_a, copy_b, k)
 
     def third(k):
         settle(part_b, recv_b, state_b, copy_b, k)
@@ -338,7 +410,6 @@
         return carry
 
     sum_lines = (along_y, along_z)
-    half_lane = lane // 2
 
     def line_copy_of(b, h, r):
         return remote(
@@ -419,7 +490,14 @@
                 vec_copy(v, r, half).wait_send()
 
     vec_drain(0)
-    pl.when(x == 0)(lambda: vec_drain(1))
+
+    @pl.when(helper)
+    def _():
+        vec_drain(1)
+        for m in range(4):
+            pass_on(m).wait_send()
+        carry_copy(0).wait_send()
+
     vec_drain(2)
     for b in range(2):
         arrow_sibling_copy(b, core).wait_send()
@@ -498,6 +576,9 @@
             pltpu.VMEM((SIDE - 1, lane, span), half),
             pltpu.VMEM((lane, span), half),
             pltpu.VMEM((lane, span), half),
+            pltpu.VMEM((2, span, span), half),
+            pltpu.VMEM((4, shard // 2, span), half),
+            pltpu.VMEM((lane // 2, span), half),
             pltpu.VMEM((blocks, effects, span), half),
             pltpu.VMEM((3, lane, shard), half),
             pltpu.VMEM((blocks, shard, lane), half),
@@ -506,6 +587,7 @@
             pltpu.VMEM((2, effects, lane // 2), full),
             pltpu.VMEM((2, 2, SIDE, effects, lane // 2), full),
             dma((5,)), dma((4, SIDE)), dma((4, SIDE)), dma((4,)), dma((4, SIDE)), dma((4, SIDE)),
+            dma((4,)), dma((4,)), dma((2,)), dma,
             dma((3,)), dma((3,)), dma((3, SIDE, 2)), dma((3, SIDE, 2)),
             dma((chunks, SIDE)), dma((chunks, SIDE)), dma((chunks, SIDE)), dma((chunks, SIDE)),
             dma((chunks,)), dma((chunks,)),

time: 138 us -> 126 us (0.913)
  Pallas kernels: 133 us -> 122 us
    pallas_call x1, Pallas kernels: 133 us -> 122 us  [body(): pl.pallas_call(kernel, out_shape=(jax.ShapeDtypeStruct(right_sides.shape,...]
where the time goes in v3:
time: 126 us
  Pallas kernels  122 us (97%)
  local copies, waits for them, and re-layouts  3.24 us (3%)
    pallas_call x1, Pallas kernels, body(): pl.pallas_call(kernel, out_shape=(jax.ShapeDtypeStruct(right_sides.shape,...  122 us
    unnamed x2, local copies, waits for them, and re-layouts  3.24 us

profile of v3, /device:TPU:1, one launch (start us, length us, event | category | flops | bytes accessed | tf_op | source)
XLA Modules:
  0.0 126.1 jit_solution(13181972508177553347)
XLA Ops:
  0.6 122.2 %shard_map.86 = (bf16[2,128,512]{2,1,0:T(8,128)(2,1)}, f32[64,512]{1,0:T(8,128)}) custom-call(bf16[2,128,512]{2,1,0:T(8,128)(2,1)} %rhs_hbm.1, bf16[2,128,4096]{2,1,0:T(8,128)(2,1)} %diag_ref.1, bf16[2,128,4096]{2,1,0:T(8,128)(2,1)} %coup_ref.1, bf16[128,512]{1,0:T(8,128)(2,1)} %carry_hbm.1, bf16[2,64,128]{2,1,0:T(8,128)(2,1)} %arrow_hbm.1, ...), custom_call_target="tpu_custom_call" | custom-call | tf_op jit(solution)/shard_map/pallas_call | solution.py:554
  122.9 1.7 %copy.11 = bf16[2,128,512]{2,1,0:T(8,128)(2,1)} copy(bf16[2,128,512]{2,1,0:T(8,128)(2,1)} %get-tuple-element.4) | data formatting | bytes 524288
  124.6 1.6 %copy.12 = f32[64,512]{1,0:T(8,128)} copy(f32[64,512]{1,0:T(8,128)} %get-tuple-element.5) | data formatting | bytes 262144

commit v4 on v3

--- a/solution.py
+++ b/solution.py
@@ -64,8 +64,6 @@
     for load in loads:
         load.start()
 
-    helper = jnp.logical_or(x == 1, x == 3)
-    part = x // 2
 
     def aligned(value, unit):
         return pl.multiple_of(value, unit)
@@ -83,7 +81,6 @@
     for target in neighbours:
         pl.semaphore_signal(barrier, inc=1, device_id=target, device_id_type=MESH)
 
-    half_lane = lane // 2
     targets = (gathered.at[0], relay_carry, gathered.at[1])
     vec_lines = (along_y, along_y, along_z)
     vec_mine = (y, y, z)
@@ -91,23 +88,17 @@
     def slot(v, at, half):
         return targets[v].at[:, pl.ds(aligned(at * chip + half * shard, shard), shard)]
 
-    def leaves(v):
-        return turned.at[v, pl.ds(0, half_lane)] if v == 1 else turned.at[v]
-
     def turn(v, value):
         value = value.T
         mine, theirs = value[:lane], value[lane:]
-        if v == 1:
-            mine = jnp.where(part == 0, mine[:half_lane], mine[half_lane:])
-            theirs = jnp.where(part == 0, theirs[:half_lane], theirs[half_lane:])
         mine, theirs = jnp.where(core == 0, mine, theirs), jnp.where(core == 0, theirs, mine)
         slot(v, vec_mine[v], core)[...] = mine
-        leaves(v)[...] = theirs
+        turned[v] = theirs
 
     loads[0].wait()
     loads[1].wait()
     turn(0, rhs_ref[0])
-    pl.when(helper)(lambda: turn(1, carry_ref[...]))
+    pl.when(x == 1)(lambda: turn(1, carry_ref[...]))
     turn(2, rhs_ref[1])
     pl.semaphore_wait(barrier, len(neighbours))
 
@@ -146,19 +137,25 @@
         rows = shard // 2
         found = pieces(m, 2)
         width = span // len(found)
-        for n, (src, _) in enumerate(found):
+        for n, (src, dst) in enumerate(found):
             columns = pl.ds(n * width, width)
-            for h, d in enumerate((1, 3)):
-                target = device(x + d, y, z + 2, core) if m < 2 else device(x + d, y + 2, z, core)
-                remote(
-                    src.at[pl.ds(h * rows, rows)], relay.at[m, :, columns],
-                    mat_send.at[m, 2], relay_recv.at[m], target,
-                ).start()
+            target = device(x + 3, y, z + 2, core) if m < 2 else device(x + 3, y + 2, z, core)
+            remote(
+                src.at[pl.ds(rows, rows)], relay.at[m, :, columns],
+                mat_send.at[m, 2], relay_recv.at[m], target,
+            ).start()
+        start = aligned(mine[m] * chip + core * shard, shard)
+        for n, (src, dst) in enumerate(found):
+            columns = pl.ds(n * width, width)
+            remote(
+                src.at[pl.ds(0, rows)], mats.at[m, pl.ds(start, rows), columns],
+                mat_send.at[m, 2], mat_recv.at[m, 2], lines[m](2),
+            ).start()
 
     def pass_on(m):
         rows = shard // 2
         at = lax.rem(mine[m] + 2, SIDE)
-        dst = mats.at[m, pl.ds(aligned(at * chip + core * shard + part * rows, rows), rows), :]
+        dst = mats.at[m, pl.ds(aligned(at * chip + core * shard + rows, rows), rows), :]
         return remote(relay.at[m], dst, relay_send.at[m], mat_recv.at[m, 2], device(0, y, z, core))
 
     def relay_wait(m):
@@ -203,7 +200,7 @@
 
     def turn_copy(v):
         return remote(
-            leaves(v), slot(v, vec_mine[v], core), turn_send.at[v], turn_recv.at[v], sibling
+            turned.at[v], slot(v, vec_mine[v], core), turn_send.at[v], turn_recv.at[v], sibling
         )
 
     def vec_copy(v, r, half):
@@ -252,50 +249,59 @@
         rows = arrow_line.at[b, :, pl.ds(aligned(at * chip, chip), chip)]
         return remote(rows, rows, arrow_send.at[b, r], arrow_recv.at[b, r], arrow_lines[b](r))
 
+    def carry_copy():
+        return remote(relay_carry, arriving, carry_send, carry_recv, device(0, y, z, core))
+
+    pl.when(x == 1)(lambda: vec_begin(1))
     vec_begin(0)
-    pl.when(helper)(lambda: vec_begin(1))
-    for m in range(2):
-        send_near(m)
 
     @pl.when(x == 0)
     def _():
         for m in range(2):
             send_round(m)
 
+    @pl.when(x < 3)
+    def _():
+        for m in range(2):
+            send_near(m)
+
     turn_copy(2).start()
+    pl.when(x == 1)(lambda: vec_rest(1))
     vec_rest(0)
-    pl.when(helper)(lambda: vec_rest(1))
-    for m in range(2, 4):
-        send_near(m)
 
     @pl.when(x == 0)
     def _():
         for m in range(2, 4):
             send_round(m)
 
+    @pl.when(x < 3)
+    def _():
+        for m in range(2, 4):
+            send_near(m)
+
+    @pl.when(jnp.logical_or(x == 1, x == 2))
+    def _():
+        for m in range(4):
+            send_far(m)
+
     for m in range(4):
         send_local(m)
 
-    def carry_copy(p):
-        return remote(
-            relay_carry, arriving.at[pl.ds(p * half_lane, half_lane)],
-            carry_send, carry_recv.at[p], device(0, y, z, core),
-        )
-
-    @pl.when(helper)
-    def _():
-        for m in range(2):
+    @pl.when(x == 1)
+    def _():
+        vec_wait(1)
+        carry_copy().start()
+
+    @pl.when(x == 3)
+    def _():
+        for m in (0, 1):
             relay_wait(m)
             pass_on(m).start()
-        vec_wait(1)
-        for p in range(2):
-            pl.when(part == p)(carry_copy(p).start)
-        for m in range(2, 4):
+        for m in (2, 3):
             relay_wait(m)
             pass_on(m).start()
-
-    @pl.when(x > 0)
-    def _():
+        for m in range(4):
+            send_near(m)
         for m in range(4):
             send_far(m)
 
@@ -305,19 +311,18 @@
         arrow_sibling_copy(b, core).start()
 
     forward(0)
+    for r in (2, 1, 3):
+        vec_copy(2, r, core).start()
+    vec_rest(2)
     vec_wait(0)
     complete(0)
     part_a[...] = times_transposed(gathered[0], mats[0])
     forward(1)
-    for r in (2, 1, 3):
-        vec_copy(2, r, core).start()
-    vec_rest(2)
     complete(1)
 
     @pl.when(x == 0)
     def _():
-        for p in range(2):
-            carry_copy(p).wait_recv()
+        carry_copy().wait_recv()
 
     def rows_of(k):
         return pl.ds(aligned(k * CHUNK, CHUNK), CHUNK)
@@ -410,6 +415,7 @@
         return carry
 
     sum_lines = (along_y, along_z)
+    half_lane = lane // 2
 
     def line_copy_of(b, h, r):
         return remote(
@@ -491,12 +497,15 @@
 
     vec_drain(0)
 
-    @pl.when(helper)
+    @pl.when(x == 1)
     def _():
         vec_drain(1)
+        carry_copy().wait_send()
+
+    @pl.when(x == 3)
+    def _():
         for m in range(4):
             pass_on(m).wait_send()
-        carry_copy(0).wait_send()
 
     vec_drain(2)
     for b in range(2):
@@ -578,7 +587,7 @@
             pltpu.VMEM((lane, span), half),
             pltpu.VMEM((2, span, span), half),
             pltpu.VMEM((4, shard // 2, span), half),
-            pltpu.VMEM((lane // 2, span), half),
+            pltpu.VMEM((lane, span), half),
             pltpu.VMEM((blocks, effects, span), half),
             pltpu.VMEM((3, lane, shard), half),
             pltpu.VMEM((blocks, shard, lane), half),
@@ -587,7 +596,7 @@
             pltpu.VMEM((2, effects, lane // 2), full),
             pltpu.VMEM((2, 2, SIDE, effects, lane // 2), full),
             dma((5,)), dma((4, SIDE)), dma((4, SIDE)), dma((4,)), dma((4, SIDE)), dma((4, SIDE)),
-            dma((4,)), dma((4,)), dma((2,)), dma,
+            dma((4,)), dma((4,)), dma, dma,
             dma((3,)), dma((3,)), dma((3, SIDE, 2)), dma((3, SIDE, 2)),
             dma((chunks, SIDE)), dma((chunks, SIDE)), dma((chunks, SIDE)), dma((chunks, SIDE)),
             dma((chunks,)), dma((chunks,)),

time: 126 us -> 123 us (0.976)
  Pallas kernels: 122 us -> 119 us
    pallas_call x1, Pallas kernels: 122 us -> 119 us  [body(): pl.pallas_call(kernel, out_shape=(jax.ShapeDtypeStruct(right_sides.shape,...]
where the time goes in v4:
time: 123 us
  Pallas kernels  119 us (97%)
  local copies, waits for them, and re-layouts  3.24 us (3%)
    pallas_call x1, Pallas kernels, body(): pl.pallas_call(kernel, out_shape=(jax.ShapeDtypeStruct(right_sides.shape,...  119 us
    unnamed x2, local copies, waits for them, and re-layouts  3.24 us

profile of v4, /device:TPU:1, one launch (start us, length us, event | category | flops | bytes accessed | tf_op | source)
XLA Modules:
  0.0 123.0 jit_solution(14233909161130709358)
XLA Ops:
  0.6 119.1 %shard_map.86 = (bf16[2,128,512]{2,1,0:T(8,128)(2,1)}, f32[64,512]{1,0:T(8,128)}) custom-call(bf16[2,128,512]{2,1,0:T(8,128)(2,1)} %rhs_hbm.1, bf16[2,128,4096]{2,1,0:T(8,128)(2,1)} %diag_ref.1, bf16[2,128,4096]{2,1,0:T(8,128)(2,1)} %coup_ref.1, bf16[128,512]{1,0:T(8,128)(2,1)} %carry_hbm.1, bf16[2,64,128]{2,1,0:T(8,128)(2,1)} %arrow_hbm.1, ...), custom_call_target="tpu_custom_call" | custom-call | tf_op jit(solution)/shard_map/pallas_call | solution.py:563
  119.7 1.7 %copy.11 = bf16[2,128,512]{2,1,0:T(8,128)(2,1)} copy(bf16[2,128,512]{2,1,0:T(8,128)(2,1)} %get-tuple-element.4) | data formatting | bytes 524288
  121.4 1.6 %copy.12 = f32[64,512]{1,0:T(8,128)} copy(f32[64,512]{1,0:T(8,128)} %get-tuple-element.5) | data formatting | bytes 262144

commit v5 on v4

--- a/solution.py
+++ b/solution.py
@@ -134,14 +134,14 @@
             remote(src, dst, mat_send.at[m, 2], mat_recv.at[m, 2], lines[m](2)).start()
 
     def send_round(m):
-        rows = shard // 2
+        rows = shard - (96, 80)[m // 2]
         found = pieces(m, 2)
         width = span // len(found)
         for n, (src, dst) in enumerate(found):
             columns = pl.ds(n * width, width)
             target = device(x + 3, y, z + 2, core) if m < 2 else device(x + 3, y + 2, z, core)
             remote(
-                src.at[pl.ds(rows, rows)], relay.at[m, :, columns],
+                src.at[pl.ds(rows, shard - rows)], relay.at[m, pl.ds(0, shard - rows), columns],
                 mat_send.at[m, 2], relay_recv.at[m], target,
             ).start()
         start = aligned(mine[m] * chip + core * shard, shard)
@@ -153,13 +153,16 @@
             ).start()
 
     def pass_on(m):
-        rows = shard // 2
-        at = lax.rem(mine[m] + 2, SIDE)
-        dst = mats.at[m, pl.ds(aligned(at * chip + core * shard + rows, rows), rows), :]
-        return remote(relay.at[m], dst, relay_send.at[m], mat_recv.at[m, 2], device(0, y, z, core))
+        rows = (96, 80)[m // 2]
+        at = lax.rem(mine[m] + 2, SIDE) * chip + core * shard + shard - rows
+        dst = mats.at[m, pl.ds(aligned(at, 16), rows), :]
+        return remote(
+            relay.at[m, pl.ds(0, rows)], dst, relay_send.at[m], mat_recv.at[m, 2], device(0, y, z, core)
+        )
 
     def relay_wait(m):
-        remote(relay.at[m], relay.at[m], relay_send.at[m], relay_recv.at[m], device(0, y, z, core)).wait_recv()
+        held = relay.at[m, pl.ds(0, (96, 80)[m // 2])]
+        remote(held, held, relay_send.at[m], relay_recv.at[m], device(0, y, z, core)).wait_recv()
 
     def send_local(m):
         for src, dst in pieces(m, 0):
@@ -586,7 +589,7 @@
             pltpu.VMEM((lane, span), half),
             pltpu.VMEM((lane, span), half),
             pltpu.VMEM((2, span, span), half),
-            pltpu.VMEM((4, shard // 2, span), half),
+            pltpu.VMEM((4, shard, span), half),
             pltpu.VMEM((lane, span), half),
             pltpu.VMEM((blocks, effects, span), half),
             pltpu.VMEM((3, lane, shard), half),

time: 123 us -> 123 us (level)
  no operation moved by 1% of the time
where the time goes in v5:
time: 123 us
  Pallas kernels  119 us (97%)
  local copies, waits for them, and re-layouts  3.24 us (3%)
    pallas_call x1, Pallas kernels, body(): pl.pallas_call(kernel, out_shape=(jax.ShapeDtypeStruct(right_sides.shape,...  119 us
    unnamed x2, local copies, waits for them, and re-layouts  3.24 us

profile of v5, /device:TPU:1, one launch (start us, length us, event | category | flops | bytes accessed | tf_op | source)
XLA Modules:
  0.0 123.0 jit_solution(14067661736531242613)
XLA Ops:
  0.6 119.1 %shard_map.86 = (bf16[2,128,512]{2,1,0:T(8,128)(2,1)}, f32[64,512]{1,0:T(8,128)}) custom-call(bf16[2,128,512]{2,1,0:T(8,128)(2,1)} %rhs_hbm.1, bf16[2,128,4096]{2,1,0:T(8,128)(2,1)} %diag_ref.1, bf16[2,128,4096]{2,1,0:T(8,128)(2,1)} %coup_ref.1, bf16[128,512]{1,0:T(8,128)(2,1)} %carry_hbm.1, bf16[2,64,128]{2,1,0:T(8,128)(2,1)} %arrow_hbm.1, ...), custom_call_target="tpu_custom_call" | custom-call | tf_op jit(solution)/shard_map/pallas_call | solution.py:566
  119.8 1.7 %copy.11 = bf16[2,128,512]{2,1,0:T(8,128)(2,1)} copy(bf16[2,128,512]{2,1,0:T(8,128)(2,1)} %get-tuple-element.4) | data formatting | bytes 524288
  121.4 1.6 %copy.12 = f32[64,512]{1,0:T(8,128)} copy(f32[64,512]{1,0:T(8,128)} %get-tuple-element.5) | data formatting | bytes 262144

commit v6 on v5

--- a/solution.py
+++ b/solution.py
@@ -330,9 +330,10 @@
     def rows_of(k):
         return pl.ds(aligned(k * CHUNK, CHUNK), CHUNK)
 
-    def chunk_copy(src, dst, send, recv, line, k, r):
-        return remote(
-            src.at[rows_of(k)], dst.at[r - 1, rows_of(k)], send.at[k, r], recv.at[k, r], line(r)
+    def chunk_copy(src, dst, send, recv, line, k, r, columns=slice(None)):
+        return remote(
+            src.at[rows_of(k), columns], dst.at[r - 1, rows_of(k), columns],
+            send.at[k, r], recv.at[k, r], line(r),
         )
 
     copy_a = functools.partial(chunk_copy, send_a, recv_a, a_send, a_recv, along_z)
@@ -345,13 +346,16 @@
 
     def spread(terms, sent, matrix, source, copy, k):
         rows = rows_of(k)
-        value = terms[rows, :] - jnp.dot(
-            source[rows, :], matrix[...], preferred_element_type=jnp.float32
-        )
-        terms[rows, :] = value
-        sent[rows, :] = value.astype(jnp.bfloat16)
-        for r in (2, 1, 3):
-            copy(k, r).start()
+        width = span // 2
+        for h in range(2):
+            columns = pl.ds(h * width, width)
+            value = terms[rows, columns] - jnp.dot(
+                source[rows, :], matrix[:, columns], preferred_element_type=jnp.float32
+            )
+            terms[rows, columns] = value
+            sent[rows, columns] = value.astype(jnp.bfloat16)
+            for r in (2, 1, 3):
+                copy(k, r, columns).start()
 
     def settle(terms, received, state, copy, k):
         rows = rows_of(k)

time: 123 us -> 123 us (level)
  no operation moved by 1% of the time
where the time goes in v6:
time: 123 us
  Pallas kernels  119 us (97%)
  local copies, waits for them, and re-layouts  3.24 us (3%)
    pallas_call x1, Pallas kernels, body(): pl.pallas_call(kernel, out_shape=(jax.ShapeDtypeStruct(right_sides.shape,...  119 us
    unnamed x2, local copies, waits for them, and re-layouts  3.24 us

profile of v6, /device:TPU:1, one launch (start us, length us, event | category | flops | bytes accessed | tf_op | source)
XLA Modules:
  0.0 123.2 jit_solution(16487292210889463216)
XLA Ops:
  0.6 119.3 %shard_map.86 = (bf16[2,128,512]{2,1,0:T(8,128)(2,1)}, f32[64,512]{1,0:T(8,128)}) custom-call(bf16[2,128,512]{2,1,0:T(8,128)(2,1)} %rhs_hbm.1, bf16[2,128,4096]{2,1,0:T(8,128)(2,1)} %diag_ref.1, bf16[2,128,4096]{2,1,0:T(8,128)(2,1)} %coup_ref.1, bf16[128,512]{1,0:T(8,128)(2,1)} %carry_hbm.1, bf16[2,64,128]{2,1,0:T(8,128)(2,1)} %arrow_hbm.1, ...), custom_call_target="tpu_custom_call" | custom-call | tf_op jit(solution)/shard_map/pallas_call | solution.py:570
  119.9 1.7 %copy.11 = bf16[2,128,512]{2,1,0:T(8,128)(2,1)} copy(bf16[2,128,512]{2,1,0:T(8,128)(2,1)} %get-tuple-element.4) | data formatting | bytes 524288
  121.6 1.6 %copy.12 = f32[64,512]{1,0:T(8,128)} copy(f32[64,512]{1,0:T(8,128)} %get-tuple-element.5) | data formatting | bytes 262144
